TPU v7x, 32 devices: a whole 2x2x4 slice. The times are simulated.
32 devices in a mesh: groups: 2 (over y), tier: 4 (over z), dir: 2 (over x), sub: 2 (over core).
Axes of the slice: x: 2, y: 2, z: 4, core: 2. Of those that a mesh axis runs over, the one named last changes fastest.
Arguments:
- auxiliary: float32 [1024, 4608], P(('groups', 'tier', 'sub')), parts along dimension 0, may hold values from -6 to 6
- hamiltonian: float32 [96, 48], P('groups'), parts along dimension 0, may hold values from -0.875 to 0.875
- coupling_re: float32 [192], P('groups'), parts along dimension 0, may hold values from 0.25 to 2
- coupling_im: float32 [192], P('groups'), parts along dimension 0, may hold values from -1 to 1
- damping_rates: float32 [192], P('groups'), parts along dimension 0, may hold values from 0.05 to 0.5
- routes: int32 [1024, 4], P(('groups', 'tier', 'sub')), parts along dimension 0, may hold values from 0 to 15, all different within a row; in each aligned block of 64 rows (0 to 63, 64 to 127, ...) at most 32 rows name the same one
- partner: int32 [1024, 4], P(('groups', 'tier', 'sub')), parts along dimension 0, may hold values from 0 to 63
- within: int32 [1024, 4], P(('groups', 'tier', 'sub')), parts along dimension 0, may hold values from 0 to 47
- levels: int32 [1024, 4], P(('groups', 'tier', 'sub')), parts along dimension 0, may hold values from 1 to 4
Outputs:
- slope_first: float32 [1024, 4608], P(('groups', 'tier', 'sub')), parts along dimension 0
- slope_second: float32 [1024, 4608], P(('groups', 'tier', 'sub')), parts along dimension 0
There are 2 independent parts, one for each index of `groups`. A program takes and returns all parts, laid end to end along the dimension named above; each array names one. Nothing has to cross between parts.
Inputs may be any that keep to these rules, and one draw needn't show every extreme that they name: `routes`: within the rows of one group (64 matrices in a row) no route number appears more than 32 times, and the 4 numbers of one matrix differ.
All inputs are finite; a program needn't handle non-finite values.
Results may differ from a plain program's by a relative error of at most 0.00005.
Values sent between devices are 32-bit elements; how exact they have to be, the bound alone decides.
A program may use at most 128 MiB of HBM per device.

v0:
```python
import jax
import jax.numpy as jnp
from jax import lax
from jax.sharding import PartitionSpec as P

precise = lax.Precision.HIGHEST
step_length = 0.2


def commutator_part(blocked, hamiltonian):
    symmetric = 0.5 * (hamiltonian + hamiltonian.T)
    count = blocked.shape[0]
    dimension = blocked.shape[2]
    cols_first = blocked.transpose(2, 0, 1, 3).reshape(dimension, -1)
    product_left = (
        jnp.dot(symmetric, cols_first, precision=precise)
        .reshape(dimension, count, 2, dimension)
        .transpose(1, 2, 0, 3)
    )
    rows_first = blocked.transpose(3, 0, 1, 2).reshape(dimension, -1)
    product_right = (
        jnp.dot(symmetric, rows_first, precision=precise)
        .reshape(dimension, count, 2, dimension)
        .transpose(1, 2, 3, 0)
    )
    difference = product_left - product_right
    return jnp.stack([difference[:, 1], -difference[:, 0]], axis=1)


def pick_strips(stacked, pigment, dimension):
    blocked = stacked.reshape(stacked.shape[:-1] + (2, dimension, dimension))
    chosen = (pigment[..., None] == jnp.arange(dimension, dtype=jnp.int32)).astype(jnp.float32)
    row_vals = jnp.einsum("...cmj,...m->...cj", blocked, chosen, precision=precise)
    col_vals = jnp.einsum("...cim,...m->...ci", blocked, chosen, precision=precise)
    return (row_vals, col_vals)


def spread(target, pigment, row_vals, col_vals, matrix_count, dimension):
    entries = target.shape[0]
    keyed = target * dimension + pigment
    keyed_hot = (
        keyed[:, None] == jnp.arange(matrix_count * dimension, dtype=jnp.int32)[None, :]
    ).astype(jnp.float32)
    row_dense = (
        jnp.dot(keyed_hot.T, row_vals.reshape(entries, -1), precision=precise)
        .reshape(matrix_count, dimension, 2, dimension)
        .transpose(0, 2, 1, 3)
    )
    col_dense = (
        jnp.dot(keyed_hot.T, col_vals.reshape(entries, -1), precision=precise)
        .reshape(matrix_count, dimension, 2, dimension)
        .transpose(0, 2, 3, 1)
    )
    return (row_dense + col_dense).reshape(matrix_count, -1)


def per_device(
    auxiliary, hamiltonian, coupling_re, coupling_im, damping_rates, routes, partner, within, levels
):
    matrix_count = auxiliary.shape[0]
    dimension = hamiltonian.shape[0]
    direction_count = coupling_re.shape[0]
    link_count = routes.shape[1]
    group_count = lax.axis_size(("tier", "sub"))
    block_count = lax.axis_size("dir")
    per_block = direction_count // block_count
    capacity = max(2, 2 * matrix_count * link_count // (group_count * block_count))
    slot_count = group_count * capacity
    block_index = lax.axis_index("dir")
    route_flat = routes.reshape(-1)
    peer_group = route_flat // block_count
    direction_block = route_flat % block_count
    direction = direction_block * per_block + within.reshape(-1)
    pigment = direction // 2
    child_index = jnp.repeat(jnp.arange(matrix_count, dtype=jnp.int32), link_count)
    in_block = (direction_block == block_index).astype(jnp.int32)
    lookup = (direction[:, None] == jnp.arange(direction_count, dtype=jnp.int32)[None, :]).astype(
        jnp.float32
    )
    tables = jnp.dot(
        lookup, jnp.stack([coupling_re, coupling_im, damping_rates], axis=1), precision=precise
    )
    coupling_real = tables[:, 0]
    coupling_imag = tables[:, 1]
    damping = tables[:, 2]
    occupation = levels.reshape(-1).astype(jnp.float32)
    decay_rate = jnp.sum((occupation * damping).reshape(matrix_count, link_count), axis=1)
    magnitude = jnp.sqrt(coupling_real * coupling_real + coupling_imag * coupling_imag)
    up_scale = jnp.sqrt(occupation * magnitude)
    down_scale = jnp.sqrt(occupation / magnitude)
    to_peer = (peer_group[:, None] == jnp.arange(group_count, dtype=jnp.int32)[None, :]).astype(
        jnp.int32
    ) * in_block[:, None]
    slot_rank = jnp.sum((jnp.cumsum(to_peer, axis=0) - to_peer) * to_peer, axis=1)
    slot_index = peer_group * capacity + slot_rank
    placed = (slot_index[:, None] == jnp.arange(slot_count, dtype=jnp.int32)[None, :]).astype(
        jnp.int32
    ) * in_block[:, None]
    placed_float = placed.astype(jnp.float32)
    slot_child = jnp.sum(placed * (child_index + 1)[:, None], axis=0) - 1
    slot_parent = jnp.sum(placed * (partner.reshape(-1) + 1)[:, None], axis=0) - 1
    slot_pigment = jnp.sum(placed * (pigment + 1)[:, None], axis=0) - 1
    slot_values = jnp.dot(
        placed_float.T,
        jnp.stack([up_scale, down_scale * coupling_real, down_scale * coupling_imag], axis=1),
        precision=precise,
    )
    sender = (slot_child[:, None] == jnp.arange(matrix_count, dtype=jnp.int32)[None, :]).astype(
        jnp.float32
    ) * slot_values[:, 0:1]
    parent_ids = slot_parent.reshape(group_count, capacity)
    parent_pigments = slot_pigment.reshape(group_count, capacity)

    def derivative(stacked):
        blocked = stacked.reshape(matrix_count, 2, dimension, dimension)
        outgoing = jnp.dot(sender, stacked, precision=precise)
        asked_ids = lax.all_to_all(
            parent_ids, ("tier", "sub"), split_axis=0, concat_axis=0, tiled=True
        )
        asked_pig = lax.all_to_all(
            parent_pigments, ("tier", "sub"), split_axis=0, concat_axis=0, tiled=True
        )
        carried = lax.all_to_all(
            outgoing.reshape(group_count, capacity, -1),
            ("tier", "sub"),
            split_axis=0,
            concat_axis=0,
            tiled=True,
        )
        wanted = (asked_ids[..., None] == jnp.arange(matrix_count, dtype=jnp.int32)).astype(
            jnp.float32
        )
        answer = jnp.einsum("gsl,ln->gsn", wanted, stacked, precision=precise)
        returned = lax.all_to_all(answer, ("tier", "sub"), split_axis=0, concat_axis=0, tiled=True)
        returned, asked_ids, asked_pig, carried = (returned, asked_ids, asked_pig, carried)
        got_rows, got_cols = pick_strips(
            carried.reshape(slot_count, -1), asked_pig.reshape(-1), dimension
        )
        far_rows, far_cols = pick_strips(returned.reshape(slot_count, -1), slot_pigment, dimension)
        up_rows = jnp.stack([got_rows[:, 1], -got_rows[:, 0]], axis=1)
        up_cols = jnp.stack([-got_cols[:, 1], got_cols[:, 0]], axis=1)
        real_part = slot_values[:, 1:2]
        imag_part = slot_values[:, 2:3]
        down_rows = jnp.stack(
            [
                real_part * far_rows[:, 1] + imag_part * far_rows[:, 0],
                -real_part * far_rows[:, 0] + imag_part * far_rows[:, 1],
            ],
            axis=1,
        )
        down_cols = jnp.stack(
            [
                -real_part * far_cols[:, 1] + imag_part * far_cols[:, 0],
                real_part * far_cols[:, 0] + imag_part * far_cols[:, 1],
            ],
            axis=1,
        )
        targets = jnp.concatenate([asked_ids.reshape(-1), slot_child])
        target_pigments = jnp.concatenate([asked_pig.reshape(-1), slot_pigment])
        all_rows = jnp.concatenate([up_rows, down_rows])
        all_cols = jnp.concatenate([up_cols, down_cols])
        partial_terms = spread(
            targets, target_pigments, all_rows, all_cols, matrix_count, dimension
        )
        coupled = lax.psum(partial_terms, "dir").reshape(matrix_count, 2, dimension, dimension)
        result = (
            commutator_part(blocked, hamiltonian)
            - decay_rate[:, None, None, None] * blocked
            + coupled
        )
        return result.reshape(matrix_count, -1)

    slope_first = derivative(auxiliary)
    slope_second = derivative(auxiliary + 0.5 * step_length * slope_first)
    return (slope_first, slope_second)


def solution(mesh):
    in_specs = (
        P(("groups", "tier", "sub"), None),
        P("groups", None),
        P("groups"),
        P("groups"),
        P("groups"),
        P(("groups", "tier", "sub"), None),
        P(("groups", "tier", "sub"), None),
        P(("groups", "tier", "sub"), None),
        P(("groups", "tier", "sub"), None),
    )
    out_specs = (P(("groups", "tier", "sub"), None), P(("groups", "tier", "sub"), None))
    return jax.shard_map(
        per_device, mesh=mesh, in_specs=in_specs, out_specs=out_specs, check_vma=False
    )
```

profile of v0, /device:TPU:0, one launch (start us, length us, event | category | flops | bytes accessed | tf_op | source)
XLA Modules:
  0.0 676.8 jit_solution(6320096181087701220)
XLA Ops:
  9.1 0.8 copy.69
  12.1 6.3 all-to-all-start
  18.5 0.8 copy.67
  19.3 0.9 fusion.81
  21.4 2.6 all-to-all-done
  23.9 3.3 all-to-all-start.1
  27.3 6.8 %fusion.74 = f32[256,4608]{1,0:T(8,128)} fusion(f32[64,4608]{1,0:T(8,128)} %param.9, f32[256]{0:T(256)S(1)} %bitcast.180, s32[256]{0:T(256)S(1)} %broadcast_add_fusion.2), kind=kOutput, calls=%fused_computation.90 | convolution fusion | flops 906002432 | bytes 5900288 | tf_op jit(solution)/shard_map/dot_general | solution.py:116
  34.1 5.1 all-to-all-start.2
  39.2 4.2 fusion.26
  43.4 101.1 %all-to-all-done.2 = f32[8,32,4608]{2,1,0:T(8,128)} async-done(((f32[8,32,4608]{2,1,0:T(8,128)}), f32[8,32,4608]{2,1,0:T(8,128)}, u32[]{:S(2)}, u32[]{:S(2)}) %all-to-all-start.2) | async-done | bytes 4718624 | tf_op jit(solution)/shard_map/all_to_all | solution.py:123
  144.6 4.6 all-to-all-start.3
  149.6 2.4 reshape.438
  152.1 1.9 copy.63
  154.0 7.2 %dot_general.102 = f32[64,2,48,48]{2,1,0,3:T(2,128)} reshape(f32[6144,48]{0,1:T(8,128)} %bitcast.163) | data formatting | bytes 2359296 | tf_op jit(solution)/shard_map/dot_general | solution.py:22
  161.2 5.7 copy.64
  166.9 3.3 copy.61
  170.2 7.0 %reshape.439 = f32[48,6144]{1,0:T(8,128)} reshape(f32[48,64,2,48]{3,2,1,0:T(2,128)} %copy.61) | data formatting | bytes 2359296 | tf_op jit(solution)/shard_map/reshape | solution.py:14
  177.2 6.1 dot_general.99
  183.2 3.4 copy.62
  188.9 10.6 %reshape_reshape.12 = f32[256,2,48,48]{3,2,1,0:T(8,128)} reshape(f32[8,32,4608]{2,1,0:T(8,128)} %all-to-all-done.2) | data formatting | bytes 9437184 | tf_op jit(solution)/shard_map/reshape;reshape | solution.py:31
  199.5 21.4 %fusion.40 = f32[256,1,2,48]{3,1,2,0:T(1,128)S(1)} fusion(f32[256,2,48,48]{3,2,1,0:T(8,128)} %reshape_reshape.12, pred[256,48,1,1]{1,0,2,3:T(32,128)(4,1)S(1)} %fusion.79), kind=kOutput, calls=%fused_computation.51 | convolution fusion | flops 14155776 | bytes 4829184 | tf_op jit(solution)/shard_map/...cim,...m->...ci/dot_general | solution.py:34
  221.0 7.3 %fusion.42 = f32[256,1,2,48]{3,1,2,0:T(1,128)S(1)} fusion(f32[256,2,48,48]{3,2,1,0:T(8,128)} %reshape_reshape.12, pred[256,48,1,1]{1,0,2,3:T(32,128)(4,1)S(1)} %fusion.79), kind=kOutput, calls=%fused_computation.53 | convolution fusion | flops 14155776 | bytes 4829184 | tf_op jit(solution)/shard_map/...cmj,...m->...cj/dot_general | solution.py:33
  228.4 26.0 %all-to-all-done.3 = f32[8,32,4608]{2,1,0:T(8,128)} async-done(((f32[8,32,4608]{2,1,0:T(8,128)}), f32[8,32,4608]{2,1,0:T(8,128)}, u32[]{:S(2)}, u32[]{:S(2)}) %all-to-all-start.3) | async-done | bytes 4718624 | tf_op jit(solution)/shard_map/all_to_all | solution.py:134
  254.4 10.6 %reshape_reshape.13 = f32[256,2,48,48]{3,2,1,0:T(8,128)} reshape(f32[8,32,4608]{2,1,0:T(8,128)} %all-to-all-done.3) | data formatting | bytes 9437184 | tf_op jit(solution)/shard_map/reshape;reshape | solution.py:31
  265.0 8.7 %fusion.34 = f32[256,1,2,48]{3,1,2,0:T(1,128)S(1)} fusion(f32[256,2,48,48]{3,2,1,0:T(8,128)} %reshape_reshape.13, pred[256,48,1,1]{1,0,2,3:T(32,128)(4,1)S(1)} %fusion.80), kind=kOutput, calls=%fused_computation.45 | convolution fusion | flops 14155776 | bytes 4829184 | tf_op jit(solution)/shard_map/...cmj,...m->...cj/dot_general | solution.py:33
  273.8 17.9 %fusion.32 = f32[256,1,2,48]{3,1,2,0:T(1,128)S(1)} fusion(f32[256,2,48,48]{3,2,1,0:T(8,128)S(1)} %copy-done.2, pred[256,48,1,1]{1,0,2,3:T(32,128)(4,1)S(1)} %fusion.80), kind=kOutput, calls=%fused_computation.43 | convolution fusion | flops 14155776 | bytes 4829184 | tf_op jit(solution)/shard_map/...cim,...m->...ci/dot_general | solution.py:34
  292.2 5.7 fusion.4
  298.0 2.8 bitcast_add_fusion.1
  300.8 3.5 reshape.448
  304.4 3.9 fusion.94
  308.3 3.0 bitcast_subtract_fusion.1
  311.6 2.9 copy.66
  314.5 4.6 stack.67
  319.4 26.9 %all-reduce.3.cloned.1.call-done = f32[64,4608]{1,0:T(8,128)} async-done(((f32[64,4608]{1,0:T(8,128)}), f32[64,4608]{1,0:T(8,128)}) %all-reduce.3.cloned.1.call-update) | async-done | bytes 1179664 | tf_op jit(solution)/shard_map/psum | solution.py:165
  346.3 2.9 multiply_add_fusion
  349.2 4.2 fusion.24
  353.4 4.6 all-to-all-start.5
  358.0 5.6 fusion.72
  363.6 99.8 %all-to-all-done.5 = f32[8,32,4608]{2,1,0:T(8,128)} async-done(((f32[8,32,4608]{2,1,0:T(8,128)}), f32[8,32,4608]{2,1,0:T(8,128)}, u32[]{:S(2)}, u32[]{:S(2)}) %all-to-all-start.5) | async-done | bytes 4718624 | tf_op jit(solution)/shard_map/all_to_all | solution.py:134
  463.4 4.6 all-to-all-start.4
  468.1 2.7 reshape.449
  470.8 5.2 copy.74
  476.0 6.2 reshape.450
  482.1 6.2 dot_general.119
  488.3 5.7 copy.75
  494.0 2.3 copy.76
  496.3 6.2 dot_general.122
  502.4 5.6 copy.77
  508.1 10.6 %reshape_reshape.15 = f32[256,2,48,48]{3,2,1,0:T(8,128)} reshape(f32[8,32,4608]{2,1,0:T(8,128)} %all-to-all-done.5) | data formatting | bytes 9437184 | tf_op jit(solution)/shard_map/reshape;reshape | solution.py:31
  518.7 9.0 %fusion.30 = f32[256,1,2,48]{3,1,2,0:T(1,128)S(1)} fusion(f32[256,2,48,48]{3,2,1,0:T(8,128)} %reshape_reshape.15, pred[256,48,1,1]{1,0,2,3:T(32,128)(4,1)S(1)} %fusion.80), kind=kOutput, calls=%fused_computation.41 | convolution fusion | flops 14155776 | bytes 4829184 | tf_op jit(solution)/shard_map/...cmj,...m->...cj/dot_general | solution.py:33
  527.7 17.9 %fusion.28 = f32[256,1,2,48]{3,1,2,0:T(1,128)S(1)} fusion(f32[256,2,48,48]{3,2,1,0:T(8,128)S(1)} %copy-done, pred[256,48,1,1]{1,0,2,3:T(32,128)(4,1)S(1)} %fusion.80), kind=kOutput, calls=%fused_computation.39 | convolution fusion | flops 14155776 | bytes 4829184 | tf_op jit(solution)/shard_map/...cim,...m->...ci/dot_general | solution.py:34
  545.6 27.6 %all-to-all-done.4 = f32[8,32,4608]{2,1,0:T(8,128)} async-done(((f32[8,32,4608]{2,1,0:T(8,128)}), f32[8,32,4608]{2,1,0:T(8,128)}, u32[]{:S(2)}, u32[]{:S(2)}) %all-to-all-start.4) | async-done | bytes 4718624 | tf_op jit(solution)/shard_map/all_to_all | solution.py:123
  573.3 10.7 %reshape_reshape.14 = f32[256,2,48,48]{3,2,1,0:T(8,128)} reshape(f32[8,32,4608]{2,1,0:T(8,128)} %all-to-all-done.4) | data formatting | bytes 9437184 | tf_op jit(solution)/shard_map/reshape;reshape | solution.py:31
  584.0 22.2 %fusion.36 = f32[256,1,2,48]{3,1,2,0:T(1,128)S(1)} fusion(f32[256,2,48,48]{3,2,1,0:T(8,128)} %reshape_reshape.14, pred[256,48,1,1]{1,0,2,3:T(32,128)(4,1)S(1)} %fusion.79), kind=kOutput, calls=%fused_computation.47 | convolution fusion | flops 14155776 | bytes 4829184 | tf_op jit(solution)/shard_map/...cim,...m->...ci/dot_general | solution.py:34
  606.2 4.4 fusion.38
  611.1 5.7 fusion
  616.9 4.5 bitcast_add_fusion
  621.4 4.8 reshape.455
  626.2 3.1 fusion.91
  629.3 3.0 bitcast_subtract_fusion
  632.6 2.9 copy.79
  635.5 3.7 stack.78
  639.3 27.9 %all-reduce.5.cloned.1.call-done = f32[64,4608]{1,0:T(8,128)} async-done(((f32[64,4608]{1,0:T(8,128)}), f32[64,4608]{1,0:T(8,128)}) %all-reduce.5.cloned.1.call-update) | async-done | bytes 1179664 | tf_op jit(solution)/shard_map/psum | solution.py:165
  667.2 2.5 subtract_add_fusion
  (90 shorter events, 10.2 us)
Async XLA Ops:
  12.1 11.8 %all-to-all-start = ((s32[8,1,32]{2,1,0:T(1,128)}), s32[8,1,32]{2,1,0:T(1,128)S(1)}, u32[]{:S(2)}, u32[]{:S(2)}) async-start(s32[8,1,32]{2,1,0:T(1,128)} %sub.48), calls=%async_computation | async-start | bytes 8192 | tf_op jit(solution)/shard_map/all_to_all | solution.py:117
  23.9 10.1 %all-to-all-start.1 = ((s32[8,1,32]{2,1,0:T(1,128)}), s32[8,1,32]{2,1,0:T(1,128)S(1)}, u32[]{:S(2)}, u32[]{:S(2)}) async-start(s32[8,1,32]{2,1,0:T(1,128)} %sub.52), calls=%async_computation.1 | async-start | bytes 8192 | tf_op jit(solution)/shard_map/all_to_all | solution.py:120
  34.1 5.1 copy-start.3
  34.1 110.5 %all-to-all-start.2 = ((f32[8,32,4608]{2,1,0:T(8,128)}), f32[8,32,4608]{2,1,0:T(8,128)}, u32[]{:S(2)}, u32[]{:S(2)}) async-start(f32[8,32,4608]{2,1,0:T(8,128)} %bitcast.159), calls=%async_computation.2 | async-start | bytes 9437184 | tf_op jit(solution)/shard_map/all_to_all | solution.py:123
  144.6 109.9 %all-to-all-start.3 = ((f32[8,32,4608]{2,1,0:T(8,128)}), f32[8,32,4608]{2,1,0:T(8,128)}, u32[]{:S(2)}, u32[]{:S(2)}) async-start(f32[8,32,4608]{2,1,0:T(8,128)} %fusion.26), calls=%async_computation.3 | async-start | bytes 9437184 | tf_op jit(solution)/shard_map/all_to_all | solution.py:134
  149.2 2.8 copy-start.10
  149.2 197.1 %all-reduce.3.cloned.1.call-start = ((), (), s32[]{:S(2)}) async-start(), calls=%async_computation.6 | async-start | bytes 2359296 | tf_op jit(solution)/shard_map/psum | solution.py:165
  186.7 121.6 %copy-start.8 = (f32[48,48]{1,0:T(8,128)}, f32[48,48]{1,0:T(8,128)S(1)}, u32[]{:S(2)}) copy-start(f32[48,48]{1,0:T(8,128)S(1)} %fusion.97) | copy-start | bytes 27652
  265.0 8.8 %copy-start.2 = (f32[256,2,48,48]{3,2,1,0:T(8,128)S(1)}, f32[256,2,48,48]{3,2,1,0:T(8,128)}, u32[]{:S(2)}) copy-start(f32[256,2,48,48]{3,2,1,0:T(8,128)} %reshape_reshape.13) | copy-start | bytes 14155780
  304.4 3.9 copy-start.6
  314.5 31.8 %copy-start.4 = (f32[64,4608]{1,0:T(8,128)S(1)}, f32[64,4608]{1,0:T(8,128)}, u32[]{:S(2)}) copy-start(f32[64,4608]{1,0:T(8,128)} %param.9) | copy-start | bytes 3538948
  353.4 110.0 %all-to-all-start.5 = ((f32[8,32,4608]{2,1,0:T(8,128)}), f32[8,32,4608]{2,1,0:T(8,128)}, u32[]{:S(2)}, u32[]{:S(2)}) async-start(f32[8,32,4608]{2,1,0:T(8,128)} %fusion.24), calls=%async_computation.5 | async-start | bytes 9437184 | tf_op jit(solution)/shard_map/all_to_all | solution.py:134
  463.4 109.9 %all-to-all-start.4 = ((f32[8,32,4608]{2,1,0:T(8,128)}), f32[8,32,4608]{2,1,0:T(8,128)}, u32[]{:S(2)}, u32[]{:S(2)}) async-start(f32[8,32,4608]{2,1,0:T(8,128)} %bitcast.158), calls=%async_computation.4 | async-start | bytes 9437184 | tf_op jit(solution)/shard_map/all_to_all | solution.py:123
  468.0 199.2 %all-reduce.5.cloned.1.call-start = ((), (), s32[]{:S(2)}) async-start(), calls=%async_computation.7 | async-start | bytes 2359296 | tf_op jit(solution)/shard_map/psum | solution.py:165
  518.7 9.0 %copy-start = (f32[256,2,48,48]{3,2,1,0:T(8,128)S(1)}, f32[256,2,48,48]{3,2,1,0:T(8,128)}, u32[]{:S(2)}) copy-start(f32[256,2,48,48]{3,2,1,0:T(8,128)} %reshape_reshape.15) | copy-start | bytes 14155780
  584.0 22.2 %copy-start.1 = (f32[256,2,48,48]{3,2,1,0:T(8,128)S(1)}, f32[256,2,48,48]{3,2,1,0:T(8,128)}, u32[]{:S(2)}) copy-start(f32[256,2,48,48]{3,2,1,0:T(8,128)} %reshape_reshape.14) | copy-start | bytes 14155780
  621.4 4.8 copy-start.5
  626.2 3.1 copy-start.7
  626.2 3.1 copy-start.9
Sparse Core Ops, SparseCore 0:
  304.5 41.7 all-reduce.2
  626.3 40.8 all-reduce.4
where the time goes:
time: 684 us; the launch traced here: 677 us
  waiting for transfers between devices  312 us (46%)
  matrix products  162 us (24%)
  local copies, waits for them, and re-layouts  149 us (22%)
  starting transfers between devices  29 us (4%)
  between operations  14.8 us (2%)
  other arithmetic  9.69 us (1%)
    all_to_all x2, waiting for transfers between devices, derivative(): lax.all_to_all(outgoing.reshape(group_count, capacity, -1), ('tier', 'sub...  129 us
    all_to_all x2, waiting for transfers between devices, derivative(): lax.all_to_all(answer, ('tier', 'sub'), split_axis=0, concat_axis=0, tile...  126 us
    dot_general x4, matrix products, pick_strips(): jnp.einsum('...cim,...m->...ci', blocked, chosen, precision=precise)  79.4 us
    psum x2, waiting for transfers between devices, derivative(): lax.psum(partial_terms, 'dir')  54.9 us
    another operation x4, local copies, waits for them, and re-layouts, pick_strips(): blocked = stacked.reshape(stacked.shape[:-1] + (2, dimension, dimension))  42.5 us
    dot_general x4, matrix products, pick_strips(): jnp.einsum('...cmj,...m->...cj', blocked, chosen, precision=precise)  29.4 us
    dot_general x4, local copies, waits for them, and re-layouts, commutator_part(): jnp.dot(symmetric, rows_first, precision=precise)  24.7 us
    dot_general x4, local copies, waits for them, and re-layouts, commutator_part(): jnp.dot(symmetric, cols_first, precision=precise)  21.3 us
  transfers between devices with their start and end apart: 8, of which 7 were waited for; matrix products, arithmetic and copies ran while one was open for 30% of the time, Pallas kernels for 0%

commit v1 on v0

v1 whole, which is shorter than its diff:
```python
import functools

import jax
import jax.numpy as jnp
from jax import lax
from jax.experimental import pallas as pl
from jax.experimental.pallas import tpu as pltpu
from jax.sharding import PartitionSpec as P

precise = lax.Precision.HIGHEST
step_length = 0.2
LANES = 128
F32 = jnp.float32
BF16 = jnp.bfloat16
MESH = pl.DeviceIdType.MESH


def iota(shape, axis):
    return lax.broadcasted_iota(jnp.int32, shape, axis)


def split(values):
    high = values.astype(BF16)
    return high, (values - high.astype(F32)).astype(BF16)


def mm(a, b):
    return jnp.dot(a, b, preferred_element_type=F32)


def exact(a, b):
    return jnp.dot(a, b, preferred_element_type=F32, precision=precise)


def swapped(strips, dim):
    lane = iota(strips.shape, 1)
    down = pltpu.roll(strips, LANES - dim, 1)
    up = pltpu.roll(strips, dim, 1)
    return jnp.where(lane < dim, down, jnp.where(lane < 2 * dim, -up, 0.0))


def turn(block, dim):
    flipped = block.T
    pad = jnp.zeros((dim, LANES - 2 * dim), F32)
    return jnp.concatenate([flipped[:dim], flipped[dim : 2 * dim], pad], axis=1)


def kernel(
    shapes, aux, weight, cols, rows, table, first, second,
    mid, dense, t_hi, t_lo, take, put, keys_out, keys_in, own_keys, sizes,
    outbox, inbox, v_hi, v_lo, rate,
    key_send, key_recv, out_send, out_recv, fwd_send, fwd_recv,
):
    count, dim, links, n, n_sub, capacity = shapes
    total = count * dim
    block = 2 * capacity
    width = 256 if n * block >= 256 else n * block
    per = width // block
    n_sets = n // per
    tall = 8 * dim

    me = lax.axis_index("tier") * n_sub + lax.axis_index("sub")
    part = lax.rem(lax.axis_index("dir"), 2)
    other = lax.axis_index("dir") + 1 - 2 * part

    def place(peer):
        return {"tier": peer // n_sub, "sub": lax.rem(peer, n_sub)}

    def peer_of(step):
        return lax.rem(me + step, n)

    barrier = pltpu.get_barrier_semaphore()

    @pl.loop(1, n)
    def _(step):
        pl.semaphore_signal(barrier, inc=1, device_id=place(peer_of(step)), device_id_type=MESH)

    pl.semaphore_signal(barrier, inc=1, device_id={"dir": other}, device_id_type=MESH)
    pl.semaphore_wait(barrier, n)

    route_col = cols[:, 0:1]
    route_row = rows[0:1, :]
    alike = route_col == route_row
    earlier = iota((links, links), 1) < iota((links, links), 0)
    later = iota((links, links), 0) < iota((links, links), 1)
    rank_col = jnp.sum(jnp.where(alike & earlier, 1.0, 0.0), axis=1, keepdims=True)
    rank_row = jnp.sum(jnp.where(alike & later, 1.0, 0.0), axis=0, keepdims=True)
    slot_col = (route_col + rank_col).astype(jnp.int32)
    slot_row = (route_row + rank_row).astype(jnp.int32)
    row_attr = rows[...]

    @pl.loop(0, n)
    def _(q):
        lane = iota((links, width), 1)
        within = slot_col - q * capacity
        inside = (within >= 0) & (within < capacity)
        mine = jnp.where((within + lax.rem(me, per) * block == lane) & inside, 1.0, 0.0)
        keys_out[q] = exact(row_attr, mine)
        kept = jnp.where((within + lax.rem(q, per) * block + capacity == lane) & inside, 1.0, 0.0)
        own_keys[q] = exact(row_attr, kept)

    def key_copy(peer, index):
        return pltpu.make_async_remote_copy(
            src_ref=keys_out.at[peer],
            dst_ref=keys_in.at[index],
            send_sem=key_send.at[peer],
            recv_sem=key_recv.at[index],
            device_id=place(peer),
            device_id_type=MESH,
        )

    @pl.loop(1, n)
    def _(step):
        key_copy(peer_of(step), me).start()

    keys_in[me] = keys_out[me]

    level = cols[:, 3:4]
    chosen = jnp.where(cols[:, 4:5].astype(jnp.int32) == iota((links, table.shape[0]), 1), 1.0, 0.0)
    found = exact(chosen, table[...])
    found = found * jnp.where(iota((links, LANES), 1) < 3, jnp.sqrt(level), level)
    owner = jnp.where(iota((count, links), 1) // (links // count) == iota((count, links), 0), 1.0, 0.0)
    rate[...] = exact(owner, found)

    @pl.loop(0, n_sets)
    def _(g):
        row = iota((width, links), 0)
        wanted = (g * per + row // block) * capacity + lax.rem(row, capacity)
        placed = jnp.where(wanted == slot_row, 1.0, 0.0)
        sizes[g] = exact(placed, found)

    def build(source):
        for m in range(dim):
            real = source[:, m * dim : (m + 1) * dim]
            imag = source[:, (dim + m) * dim : (dim + m + 1) * dim]
            pad = jnp.zeros((count, LANES - 2 * dim), F32)
            dense[pl.ds(m, count, stride=dim), :] = jnp.concatenate([real, imag, pad], axis=1)

        @pl.loop(0, count // 8)
        def _(chunk):
            for k in range(8):
                at = pl.ds(pl.multiple_of(chunk * tall + k * dim, 16), dim)
                straight = dense[at, :]
                t_hi[0, at, :], t_lo[0, at, :] = split(straight)
                t_hi[1, at, :], t_lo[1, at, :] = split(turn(straight, dim))

    build(aux)
    weight_hi, weight_lo = split(weight[...])

    @pl.loop(1, n)
    def _(step):
        key_copy(me, peer_of(step)).wait_recv()

    @pl.loop(0, n_sets)
    def _(g):
        key = jnp.zeros((8, width), F32)
        for k in range(per):
            at = g * per + k
            key = key + jnp.broadcast_to(keys_in[at][1:2], (8, width))
            key = key + jnp.broadcast_to(own_keys[at][2:3], (8, width))
        as_row = key[0:1].astype(jnp.int32) - 1
        as_col = key.T[:, 0:1].astype(jnp.int32) - 1

        @pl.loop(0, total // tall)
        def _(chunk):
            at = pl.multiple_of(chunk * tall, LANES)
            below = iota((tall, width), 0) + at
            put[g, pl.ds(at, tall), :] = jnp.where(below == as_row, 1.0, 0.0).astype(BF16)
            across = iota((width, tall), 1) + at
            take[g, :, pl.ds(at, tall)] = jnp.where(across == as_col, 1.0, 0.0).astype(BF16)

    @pl.loop(1, n)
    def _(step):
        key_copy(peer_of(step), me).wait_send()

    sign = (1 - 2 * part).astype(F32)

    def out_copy(turn_no, peer, index):
        return pltpu.make_async_remote_copy(
            src_ref=outbox.at[turn_no, peer],
            dst_ref=inbox.at[turn_no, part, index],
            send_sem=out_send.at[turn_no, peer],
            recv_sem=out_recv.at[turn_no, index],
            device_id=place(peer),
            device_id_type=MESH,
        )

    def forward(turn_no, index, which):
        return pltpu.make_async_remote_copy(
            src_ref=inbox.at[turn_no, which, index],
            dst_ref=inbox.at[turn_no, which, index],
            send_sem=fwd_send.at[turn_no, index],
            recv_sem=fwd_recv.at[turn_no, index],
            device_id={"dir": other},
            device_id_type=MESH,
        )

    def section(turn_no, source, target):
        @pl.loop(0, n_sets)
        def _(g):
            one_hot = take[g]
            strips = mm(one_hot, t_hi[part]) + mm(one_hot, t_lo[part])
            upper = (sign * sizes[g][:, 0:1]) * swapped(strips, dim)
            for k in range(per):
                at = g * per + k
                outbox[turn_no, at, 0:capacity] = upper[k * block + capacity : (k + 1) * block]
                outbox[turn_no, at, capacity:block] = strips[k * block : k * block + capacity]

                @pl.when(at != me)
                def _():
                    out_copy(turn_no, at, me).start()

        inbox[turn_no, part, me] = outbox[turn_no, me]
        forward(turn_no, me, part).start()

        @pl.loop(1, n)
        def _(step):
            peer = peer_of(step)
            out_copy(turn_no, me, peer).wait_recv()
            forward(turn_no, peer, part).start()

        @pl.loop(0, n)
        def _(q):
            forward(turn_no, q, 1 - part).wait_recv()

        @pl.loop(0, n_sets)
        def _(g):
            size = sizes[g]
            below = lax.rem(iota((width, LANES), 0), block) >= capacity
            for side in range(2):
                got = jnp.concatenate([inbox[turn_no, side, g * per + k] for k in range(per)], axis=0)
                lower = (1 - 2 * side) * size[:, 1:2] * swapped(got, dim) + size[:, 2:3] * got
                high, low = split(jnp.where(below, lower, got))
                v_hi[g, :, side * LANES : (side + 1) * LANES] = high
                v_lo[g, :, side * LANES : (side + 1) * LANES] = low

        @pl.loop(0, count // 8)
        def _(chunk):
            at = pl.ds(pl.multiple_of(chunk * tall, LANES), tall)
            spread = jnp.zeros((tall, 2 * LANES), F32)
            for g in range(n_sets):
                one_hot = put[g, at, :]
                spread = spread + mm(one_hot, v_hi[g]) + mm(one_hot, v_lo[g])
            own = []
            for side in range(2):
                high, low = t_hi[side, at, :], t_lo[side, at, :]
                own.append(mm(high, weight_hi) + mm(low, weight_hi) + mm(high, weight_lo))
            straight = spread[:, :LANES] + own[0]
            crossed = spread[:, LANES:] - own[1]
            for k in range(8):
                turned = turn(crossed[k * dim : (k + 1) * dim], dim)
                to = pl.ds(pl.multiple_of(chunk * tall + k * dim, 16), dim)
                dense[to, :] = straight[k * dim : (k + 1) * dim] + turned

        for c in range(dim // 8):
            picked = [dense[pl.ds(c * 8 + k, count, stride=dim), :] for k in range(8)]
            for half in range(2):
                at = slice((half * dim + c * 8) * dim, (half * dim + c * 8 + 8) * dim)
                flat = jnp.concatenate([p[:, half * dim : (half + 1) * dim] for p in picked], axis=1)
                target[:, at] = flat - rate[:, 3:4] * source[:, at]

        @pl.loop(1, n)
        def _(step):
            out_copy(turn_no, peer_of(step), me).wait_send()

        @pl.loop(0, n)
        def _(q):
            forward(turn_no, q, part).wait_send()

    section(0, aux, first)
    mid[...] = aux[...] + (0.5 * step_length) * first[...]
    build(mid)
    section(1, mid, second)


def per_device(
    auxiliary, hamiltonian, coupling_re, coupling_im, damping_rates, routes, partner, within, levels
):
    count, entries = auxiliary.shape
    dim = hamiltonian.shape[0]
    direction_count = coupling_re.shape[0]
    per_row = routes.shape[1]
    links = count * per_row
    n = lax.axis_size(("tier", "sub"))
    blocks = lax.axis_size("dir")
    per_block = direction_count // blocks
    each = max(2, 2 * links // (n * blocks))
    capacity = each * blocks
    block = 2 * capacity
    width = min(256, n * block)
    n_sets = n * block // width

    direction = (routes % blocks) * per_block + within
    pigment = direction // 2
    child = jnp.arange(count, dtype=jnp.int32)[:, None] * dim + pigment
    attributes = jnp.stack(
        [routes * each, partner * dim + pigment + 1, child + 1, levels, direction] + [levels] * 3, axis=-1
    )
    attributes = attributes.reshape(links, 8).astype(F32)
    root = jnp.sqrt(jnp.sqrt(coupling_re * coupling_re + coupling_im * coupling_im))
    table = jnp.stack([root, coupling_re / root, coupling_im / root, damping_rates], axis=1)
    table = jnp.pad(table, ((0, 0), (0, LANES - 4)))
    symmetric = 0.5 * (hamiltonian + hamiltonian.T)
    zero = jnp.zeros_like(symmetric)
    weight = jnp.concatenate(
        [jnp.concatenate([zero, symmetric], axis=1), jnp.concatenate([-symmetric, zero], axis=1)], axis=0
    )
    weight = jnp.pad(weight, ((0, LANES - 2 * dim), (0, LANES - 2 * dim)))

    total = count * dim
    shapes = (count, dim, links, n, lax.axis_size("sub"), capacity)
    vmem = pl.BlockSpec(memory_space=pltpu.VMEM)
    dma = pltpu.SemaphoreType.DMA
    out = jax.ShapeDtypeStruct((count, entries), F32)
    return pl.pallas_call(
        functools.partial(kernel, shapes),
        out_shape=(out, out),
        in_specs=[vmem] * 5,
        out_specs=(vmem, vmem),
        scratch_shapes=[
            pltpu.VMEM((count, entries), F32),
            pltpu.VMEM((total, LANES), F32),
            pltpu.VMEM((2, total, LANES), BF16),
            pltpu.VMEM((2, total, LANES), BF16),
            pltpu.VMEM((n_sets, width, total), BF16),
            pltpu.VMEM((n_sets, total, width), BF16),
            pltpu.VMEM((n, 8, width), F32),
            pltpu.VMEM((n, 8, width), F32),
            pltpu.VMEM((n, 8, width), F32),
            pltpu.VMEM((n_sets, width, LANES), F32),
            pltpu.VMEM((2, n, block, LANES), F32),
            pltpu.VMEM((2, 2, n, block, LANES), F32),
            pltpu.VMEM((n_sets, width, 2 * LANES), BF16),
            pltpu.VMEM((n_sets, width, 2 * LANES), BF16),
            pltpu.VMEM((count, LANES), F32),
            dma((n,)),
            dma((n,)),
            dma((2, n)),
            dma((2, n)),
            dma((2, n)),
            dma((2, n)),
        ],
        compiler_params=pltpu.CompilerParams(
            collective_id=0, has_side_effects=True, vmem_limit_bytes=56 * 1024 * 1024
        ),
        cost_estimate=pl.CostEstimate(
            flops=10**10, bytes_accessed=6 * count * entries * 4, transcendentals=0
        ),
    )(auxiliary, weight, attributes, attributes.T, table)


def solution(mesh):
    split_all = P(("groups", "tier", "sub"), None)
    in_specs = (
        split_all,
        P("groups", None),
        P("groups"),
        P("groups"),
        P("groups"),
        split_all,
        split_all,
        split_all,
        split_all,
    )
    return jax.shard_map(
        per_device, mesh=mesh, in_specs=in_specs, out_specs=(split_all, split_all), check_vma=False
    )
```

time: 684 us -> 104 us (0.15)
  the two profiles are of different devices: /device:TPU:0 before, /device:TPU:9 now
where the time goes in v1:
time: 104 us
  Pallas kernels  90 us (87%)
  local copies, waits for them, and re-layouts  8.16 us (8%)
  other arithmetic  4.87 us (5%)
    pallas_call x1, Pallas kernels, per_device(): pl.pallas_call(functools.partial(kernel, shapes), out_shape=(out, out), i...  90 us
    unnamed x6, local copies, waits for them, and re-layouts  5.06 us

profile of v1, /device:TPU:9, one launch (start us, length us, event | category | flops | bytes accessed | tf_op | source)
XLA Modules:
  0.0 103.7 jit_solution(980808363888162832)
XLA Ops:
  0.6 0.7 divide_bitcast_fusion.1
  1.3 0.7 divide_bitcast_fusion
  2.0 0.7 pad_maximum_fusion
  2.7 0.7 add_add_fusion
  3.4 0.7 add_add_fusion.1
  4.1 0.8 copy.33
  4.9 0.8 fusion.7
  5.6 0.1 select_maximum_fusion
  5.7 0.6 pad.10.weight
  6.4 0.1 copy.38
  6.5 0.1 stack.40
  6.6 0.1 copy.35
  6.7 0.1 stack.37
  6.8 0.1 copy.36
  6.9 0.1 stack.38
  7.0 0.1 copy.34
  7.1 0.1 stack.36
  7.2 0.8 copy.37
  8.0 0.1 stack.39
  8.1 0.6 convert_bitcast_fusion
  8.7 0.1 copy.39
  8.8 0.6 pad.11.table
  9.4 0.8 copy.40.cols
  10.2 90.0 %shard_map.104 = (f32[64,4608]{1,0:T(8,128)}, f32[64,4608]{1,0:T(8,128)}) custom-call(f32[64,4608]{1,0:T(8,128)} %aux.1, f32[128,128]{1,0:T(8,128)} %pad.10.weight, f32[256,8]{1,0:T(8,128)} %copy.40.cols, f32[8,256]{1,0:T(8,128)} %get-tuple-element.8.rows, f32[96,128]{1,0:T(8,128)} %pad.11.table), custom_call_target="tpu_custom_call" | custom-call | flops 10000000000 | bytes 7077888 | tf_op jit(solution)/shard_map/pallas_call | solution.py:315
  100.2 0.0 copy-start
  100.2 2.5 %copy.43 = f32[64,4608]{1,0:T(8,128)} copy(f32[64,4608]{1,0:T(8,128)} %get-tuple-element.13) | data formatting | bytes 2359296
  102.7 0.0 copy-done
  102.7 1.0 copy.44
  (2 shorter events, 0.0 us)
Async XLA Ops:
  100.2 2.5 %copy-start = (f32[64,4608]{1,0:T(8,128)S(1)}, f32[64,4608]{1,0:T(8,128)}, u32[]{:S(2)}) copy-start(f32[64,4608]{1,0:T(8,128)} %get-tuple-element.14) | copy-start | bytes 3538948

commit v2 on v1

v2 whole, which is shorter than its diff:
```python
import functools

import jax
import jax.numpy as jnp
from jax import lax
from jax.experimental import pallas as pl
from jax.experimental.pallas import tpu as pltpu
from jax.sharding import PartitionSpec as P

precise = lax.Precision.HIGHEST
step_length = 0.2
LANES = 128
F32 = jnp.float32
BF16 = jnp.bfloat16
MESH = pl.DeviceIdType.MESH


def iota(shape, axis):
    return lax.broadcasted_iota(jnp.int32, shape, axis)


def split(values):
    high = values.astype(BF16)
    return high, (values - high.astype(F32)).astype(BF16)


def mm(a, b):
    return jnp.dot(a, b, preferred_element_type=F32)


def exact(a, b):
    return jnp.dot(a, b, preferred_element_type=F32, precision=precise)


def swapped(strips, dim):
    lane = iota(strips.shape, 1)
    down = pltpu.roll(strips, LANES - dim, 1)
    up = pltpu.roll(strips, dim, 1)
    return jnp.where(lane < dim, down, jnp.where(lane < 2 * dim, -up, 0.0))


def turn(block, dim):
    flipped = block.T
    pad = jnp.zeros((dim, LANES - 2 * dim), F32)
    return jnp.concatenate([flipped[:dim], flipped[dim : 2 * dim], pad], axis=1)


def kernel(
    shapes, aux, hamiltonian, baths, links_in, first, second,
    mid, dense, own, t_hi, t_lo, take, put, keys_out, keys_in, own_keys, sizes,
    outbox, inbox, v_hi, v_lo, rate,
    key_send, key_recv, out_send, out_recv, fwd_send, fwd_recv,
):
    count, dim, links, n, n_sub, blocks, each = shapes
    capacity = each * blocks
    total = count * dim
    block = 2 * capacity
    width = 256 if n * block >= 256 else n * block
    per = width // block
    n_sets = n // per
    tall = 8 * dim
    packed = outbox.shape[2]
    third = LANES // 4

    me = lax.axis_index("tier") * n_sub + lax.axis_index("sub")
    part = lax.rem(lax.axis_index("dir"), 2)
    other = lax.axis_index("dir") + 1 - 2 * part

    def place(peer):
        return {"tier": peer // n_sub, "sub": lax.rem(peer, n_sub)}

    def peer_of(step):
        return lax.rem(me + step, n)

    barrier = pltpu.get_barrier_semaphore()

    @pl.loop(1, n)
    def _(step):
        pl.semaphore_signal(barrier, inc=1, device_id=place(peer_of(step)), device_id_type=MESH)

    pl.semaphore_signal(barrier, inc=1, device_id={"dir": other}, device_id_type=MESH)
    pl.semaphore_wait(barrier, n)

    per_row = links // count

    def row_of(which):
        at = which * per_row
        return jnp.concatenate([links_in[at + k : at + k + 1, :] for k in range(per_row)], axis=1)

    kinds = [row_of(which).astype(F32) for which in range(4)]
    columns = jnp.concatenate(kinds + kinds, axis=0).T
    route_row, route_col = kinds[0], columns[:, 0:1]
    alike = route_col == route_row
    earlier = iota((links, links), 1) < iota((links, links), 0)
    later = iota((links, links), 0) < iota((links, links), 1)
    rank_col = jnp.sum(jnp.where(alike & earlier, 1.0, 0.0), axis=1, keepdims=True)
    rank_row = jnp.sum(jnp.where(alike & later, 1.0, 0.0), axis=0, keepdims=True)
    slot_col = (route_col * each + rank_col).astype(jnp.int32)
    slot_row = (route_row * each + rank_row).astype(jnp.int32)
    bath_count = baths.shape[1]
    integers = columns.astype(jnp.int32)
    direction = (integers[:, 0:1] & (blocks - 1)) * (bath_count // blocks) + integers[:, 2:3]
    pigment = lax.shift_right_logical(direction, 1)
    parent_key = (integers[:, 1:2] * dim + pigment + 1).astype(F32)
    child_key = (lax.rem(iota((links, 1), 0), count) * dim + pigment + 1).astype(F32)

    @pl.loop(0, n)
    def _(q):
        lane = iota((links, width), 1)
        within = slot_col - q * capacity
        inside = (within >= 0) & (within < capacity)
        there = jnp.where(inside, within + lax.rem(me, per) * block, -1)
        here = jnp.where(inside, within + lax.rem(q, per) * block + capacity, -1)
        sent = jnp.sum(jnp.where(there == lane, parent_key, 0.0), axis=0, keepdims=True)
        kept = jnp.sum(jnp.where(here == lane, child_key, 0.0), axis=0, keepdims=True)
        keys_out[q] = jnp.broadcast_to(sent, (8, width))
        own_keys[q] = jnp.broadcast_to(kept, (8, width))

    def key_copy(peer, index):
        return pltpu.make_async_remote_copy(
            src_ref=keys_out.at[peer],
            dst_ref=keys_in.at[index],
            send_sem=key_send.at[peer],
            recv_sem=key_recv.at[index],
            device_id=place(peer),
            device_id_type=MESH,
        )

    @pl.loop(1, n)
    def _(step):
        key_copy(peer_of(step), me).start()

    keys_in[me] = keys_out[me]

    level = columns[:, 3:4]
    chosen = direction == iota((links, bath_count), 1)

    def pick(row):
        return jnp.sum(jnp.where(chosen, row, 0.0), axis=1, keepdims=True)

    real, imag = baths[0:1, :], baths[1:2, :]
    root = jnp.sqrt(jnp.sqrt(real * real + imag * imag))
    size_root = jnp.sqrt(level)
    scales = [size_root * pick(root), size_root * pick(real / root), size_root * pick(imag / root)]
    scales.append(level * pick(baths[2:3, :]))
    lane = iota((links, LANES), 1)
    found = jnp.zeros((links, LANES), F32)
    for which, scale in enumerate(scales):
        found = jnp.where(lane == which, scale, found)
    both = jnp.concatenate(split(found), axis=1)
    owner = jnp.where(lax.rem(iota((count, links), 1), count) == iota((count, links), 0), 1.0, 0.0)
    rates = mm(owner.astype(BF16), both)
    rate[...] = rates[:, :LANES] + rates[:, LANES:]

    @pl.loop(0, n_sets)
    def _(g):
        row = iota((width, 1), 0)
        wanted = (g * per + row // block) * capacity + lax.rem(row, capacity)
        placed = jnp.where(wanted == slot_row, 1.0, 0.0).astype(BF16)
        size = mm(placed, both)
        sizes[g] = size[:, :LANES] + size[:, LANES:]

    def build(source):
        for m in range(dim):
            real = source[:, m * dim : (m + 1) * dim]
            imag = source[:, (dim + m) * dim : (dim + m + 1) * dim]
            pad = jnp.zeros((count, LANES - 2 * dim), F32)
            dense[pl.ds(m, count, stride=dim), :] = jnp.concatenate([real, imag, pad], axis=1)

        @pl.loop(0, count // 8)
        def _(chunk):
            for k in range(8):
                at = pl.ds(pl.multiple_of(chunk * tall + k * dim, 16), dim)
                straight = dense[at, :]
                t_hi[0, at, :], t_lo[0, at, :] = split(straight)
                t_hi[1, at, :], t_lo[1, at, :] = split(turn(straight, dim))

    build(aux)
    symmetric = 0.5 * (hamiltonian[...] + hamiltonian[...].T)
    zero = jnp.zeros((dim, dim), F32)
    side_pad = jnp.zeros((dim, LANES - 2 * dim), F32)
    weight = jnp.concatenate(
        [
            jnp.concatenate([zero, symmetric, side_pad], axis=1),
            jnp.concatenate([-symmetric, zero, side_pad], axis=1),
            jnp.zeros((LANES - 2 * dim, LANES), F32),
        ],
        axis=0,
    )
    weight_hi, weight_lo = split(weight)

    @pl.loop(1, n)
    def _(step):
        key_copy(me, peer_of(step)).wait_recv()

    @pl.loop(0, n_sets)
    def _(g):
        key = jnp.zeros((8, width), F32)
        for k in range(per):
            at = g * per + k
            key = key + jnp.broadcast_to(keys_in[at][0:1], (8, width))
            key = key + jnp.broadcast_to(own_keys[at][0:1], (8, width))
        as_row = key[0:1].astype(jnp.int32) - 1
        as_col = key.T[:, 0:1].astype(jnp.int32) - 1

        @pl.loop(0, total // tall)
        def _(chunk):
            at = pl.multiple_of(chunk * tall, LANES)
            put[g, pl.ds(at, tall), :] = jnp.where(iota((tall, width), 0) == as_row - at, 1.0, 0.0).astype(BF16)
            take[g, :, pl.ds(at, tall)] = jnp.where(iota((width, tall), 1) == as_col - at, 1.0, 0.0).astype(BF16)

    @pl.loop(1, n)
    def _(step):
        key_copy(peer_of(step), me).wait_send()

    sign = (1 - 2 * part).astype(F32)

    def out_copy(turn_no, peer, index):
        return pltpu.make_async_remote_copy(
            src_ref=outbox.at[turn_no, peer],
            dst_ref=inbox.at[turn_no, part, index],
            send_sem=out_send.at[turn_no, peer],
            recv_sem=out_recv.at[turn_no, index],
            device_id=place(peer),
            device_id_type=MESH,
        )

    def forward(turn_no, index, which):
        return pltpu.make_async_remote_copy(
            src_ref=inbox.at[turn_no, which, index],
            dst_ref=inbox.at[turn_no, which, index],
            send_sem=fwd_send.at[turn_no, index],
            recv_sem=fwd_recv.at[turn_no, index],
            device_id={"dir": other},
            device_id_type=MESH,
        )

    def packing(message):
        if packed == block:
            return message
        lane = iota((packed, LANES), 1)
        last = message[packed:]
        moved = [pltpu.roll(last, LANES - third * (k + 1), 1) for k in range(3)]
        return jnp.where(lane < 3 * third, message[:packed], jnp.concatenate(moved, axis=0))

    def unpacking(message):
        if packed == block:
            return message
        quarter = block // 4
        lane = iota((quarter, LANES), 1)
        last = jnp.zeros((quarter, LANES), F32)
        for k in range(3):
            piece = pltpu.roll(message[k * quarter : (k + 1) * quarter], third * (k + 1), 1)
            last = jnp.where((lane >= k * third) & (lane < (k + 1) * third), piece, last)
        clean = jnp.where(iota((packed, LANES), 1) < 3 * third, message, 0.0)
        return jnp.concatenate([clean, last], axis=0)

    home = me // per

    def section(turn_no, source, target):
        @pl.loop(0, n_sets)
        def _(k):
            g = lax.rem(home + k, n_sets)
            one_hot = take[g]
            strips = mm(one_hot, t_hi[part]) + mm(one_hot, t_lo[part])
            upper = (sign * sizes[g][:, 0:1]) * swapped(strips, dim)
            for k in range(per):
                at = g * per + k
                outbox[turn_no, at] = packing(
                    jnp.concatenate(
                        [
                            upper[k * block + capacity : (k + 1) * block],
                            strips[k * block : k * block + capacity],
                        ],
                        axis=0,
                    )
                )

                @pl.when(at != me)
                def _():
                    out_copy(turn_no, at, me).start()

                @pl.when(at == me)
                def _():
                    inbox[turn_no, part, me] = outbox[turn_no, me]
                    forward(turn_no, me, part).start()

        @pl.loop(0, count // 8)
        def _(chunk):
            at = pl.ds(pl.multiple_of(chunk * tall, LANES), tall)
            for side in range(2):
                high, low = t_hi[side, at, :], t_lo[side, at, :]
                product = mm(high, weight_hi) + mm(low, weight_hi) + mm(high, weight_lo)
                own[at, side * LANES : (side + 1) * LANES] = -product if side else product

        def arrive(k):
            g = lax.rem(home + n_sets - k, n_sets)

            @pl.loop(0, per)
            def _(i):
                peer = g * per + i

                @pl.when(peer != me)
                def _():
                    out_copy(turn_no, me, peer).wait_recv()
                    forward(turn_no, peer, part).start()

        arrive(0)
        for k in range(n_sets):
            if k < n_sets - 1:
                arrive(k + 1)
            g = lax.rem(home + n_sets - k, n_sets)

            @pl.loop(0, per)
            def _(i):
                forward(turn_no, g * per + i, 1 - part).wait_recv()

            size = sizes[g]
            below = lax.rem(iota((width, LANES), 0), block) >= capacity
            for side in range(2):
                got = [unpacking(inbox[turn_no, side, g * per + i]) for i in range(per)]
                got = jnp.concatenate(got, axis=0)
                lower = (1 - 2 * side) * size[:, 1:2] * swapped(got, dim) + size[:, 2:3] * got
                high, low = split(jnp.where(below, lower, got))
                v_hi[:, side * LANES : (side + 1) * LANES] = high
                v_lo[:, side * LANES : (side + 1) * LANES] = low

            @pl.loop(0, count // 8)
            def _(chunk):
                at = pl.ds(pl.multiple_of(chunk * tall, LANES), tall)
                one_hot = put[g, at, :]
                value = own[at, :] + mm(one_hot, v_hi[...]) + mm(one_hot, v_lo[...])
                if k < n_sets - 1:
                    own[at, :] = value
                else:
                    for j in range(8):
                        rows = slice(j * dim, (j + 1) * dim)
                        to = pl.ds(pl.multiple_of(chunk * tall + j * dim, 16), dim)
                        dense[to, :] = value[rows, :LANES] + turn(value[rows, LANES:], dim)

        for c in range(dim // 8):
            picked = [dense[pl.ds(c * 8 + k, count, stride=dim), :] for k in range(8)]
            for half in range(2):
                at = slice((half * dim + c * 8) * dim, (half * dim + c * 8 + 8) * dim)
                flat = jnp.concatenate([p[:, half * dim : (half + 1) * dim] for p in picked], axis=1)
                target[:, at] = flat - rate[:, 3:4] * source[:, at]

        @pl.loop(1, n)
        def _(step):
            out_copy(turn_no, peer_of(step), me).wait_send()

        @pl.loop(0, n)
        def _(q):
            forward(turn_no, q, part).wait_send()

    section(0, aux, first)
    mid[...] = aux[...] + (0.5 * step_length) * first[...]
    build(mid)
    section(1, mid, second)


def per_device(
    auxiliary, hamiltonian, coupling_re, coupling_im, damping_rates, routes, partner, within, levels
):
    count, entries = auxiliary.shape
    dim = hamiltonian.shape[0]
    per_row = routes.shape[1]
    links = count * per_row
    n = lax.axis_size(("tier", "sub"))
    blocks = lax.axis_size("dir")
    each = max(2, 2 * links // (n * blocks))
    capacity = each * blocks
    block = 2 * capacity
    width = min(256, n * block)
    n_sets = n * block // width
    packed = block * 3 // 4 if block % 32 == 0 and 2 * dim == LANES * 3 // 4 else block

    links_in = jnp.concatenate([routes.T, partner.T, within.T, levels.T], axis=0)
    baths = jnp.stack([coupling_re, coupling_im, damping_rates])

    total = count * dim
    shapes = (count, dim, links, n, lax.axis_size("sub"), blocks, each)
    vmem = pl.BlockSpec(memory_space=pltpu.VMEM)
    dma = pltpu.SemaphoreType.DMA
    out = jax.ShapeDtypeStruct((count, entries), F32)
    return pl.pallas_call(
        functools.partial(kernel, shapes),
        out_shape=(out, out),
        in_specs=[vmem] * 4,
        out_specs=(vmem, vmem),
        scratch_shapes=[
            pltpu.VMEM((count, entries), F32),
            pltpu.VMEM((total, LANES), F32),
            pltpu.VMEM((total, 2 * LANES), F32),
            pltpu.VMEM((2, total, LANES), BF16),
            pltpu.VMEM((2, total, LANES), BF16),
            pltpu.VMEM((n_sets, width, total), BF16),
            pltpu.VMEM((n_sets, total, width), BF16),
            pltpu.VMEM((n, 8, width), F32),
            pltpu.VMEM((n, 8, width), F32),
            pltpu.VMEM((n, 8, width), F32),
            pltpu.VMEM((n_sets, width, LANES), F32),
            pltpu.VMEM((2, n, packed, LANES), F32),
            pltpu.VMEM((2, 2, n, packed, LANES), F32),
            pltpu.VMEM((width, 2 * LANES), BF16),
            pltpu.VMEM((width, 2 * LANES), BF16),
            pltpu.VMEM((count, LANES), F32),
            dma((n,)),
            dma((n,)),
            dma((2, n)),
            dma((2, n)),
            dma((2, n)),
            dma((2, n)),
        ],
        compiler_params=pltpu.CompilerParams(
            collective_id=0, has_side_effects=True, vmem_limit_bytes=56 * 1024 * 1024
        ),
        cost_estimate=pl.CostEstimate(
            flops=10**10, bytes_accessed=6 * count * entries * 4, transcendentals=0
        ),
    )(auxiliary, hamiltonian, baths, links_in)


def solution(mesh):
    split_all = P(("groups", "tier", "sub"), None)
    in_specs = (
        split_all,
        P("groups", None),
        P("groups"),
        P("groups"),
        P("groups"),
        split_all,
        split_all,
        split_all,
        split_all,
    )
    return jax.shard_map(
        per_device, mesh=mesh, in_specs=in_specs, out_specs=(split_all, split_all), check_vma=False
    )
```

time: 104 us -> 82 us (0.79)
  the two profiles are of different devices: /device:TPU:9 before, /device:TPU:0 now
where the time goes in v2:
time: 82 us; the launch traced here: 81.8 us
  Pallas kernels  75 us (91%)
  local copies, waits for them, and re-layouts  3.48 us (4%)
  other arithmetic  2.61 us (3%)
    pallas_call x1, Pallas kernels, per_device(): pl.pallas_call(functools.partial(kernel, shapes), out_shape=(out, out), i...  75 us
    unnamed x4, local copies, waits for them, and re-layouts  3.48 us

profile of v2, /device:TPU:0, one launch (start us, length us, event | category | flops | bytes accessed | tf_op | source)
XLA Modules:
  0.0 81.8 jit_solution(1531643224525129717)
XLA Ops:
  0.6 1.3 %pad_maximum_fusion.baths = f32[3,96]{1,0:T(4,128)} fusion(f32[1,96]{1,0:T(1,128)} %bitcast.11, f32[1,96]{1,0:T(1,128)} %bitcast.12, f32[1,96]{1,0:T(1,128)} %bitcast.13), kind=kLoop, calls=%fused_computation.1 | loop fusion | flops 576 | bytes 2304 | tf_op jit(solution)/shard_map/stack | solution.py:379
  1.9 1.3 %pad_add_fusion.links_in = s32[16,64]{1,0:T(8,128)} fusion(s32[4,64]{1,0:T(4,128)} %bitcast.7, s32[4,64]{1,0:T(4,128)} %bitcast.8, s32[4,64]{1,0:T(4,128)} %bitcast.9, s32[4,64]{1,0:T(4,128)} %bitcast.10), kind=kLoop, calls=%fused_computation | loop fusion | flops 3072 | bytes 8192 | tf_op jit(solution)/shard_map/concatenate | solution.py:378
  3.2 75.0 %shard_map.104 = (f32[64,4608]{1,0:T(8,128)}, f32[64,4608]{1,0:T(8,128)}) custom-call(f32[64,4608]{1,0:T(8,128)} %aux.1, f32[48,48]{1,0:T(8,128)} %hamiltonian.1, f32[3,96]{1,0:T(4,128)} %pad_maximum_fusion.baths, s32[16,64]{1,0:T(8,128)} %pad_add_fusion.links_in), custom_call_target="tpu_custom_call" | custom-call | flops 10000000000 | bytes 7077888 | tf_op jit(solution)/shard_map/pallas_call | solution.py:386
  78.3 0.0 copy-start
  78.3 2.5 %copy.13 = f32[64,4608]{1,0:T(8,128)} copy(f32[64,4608]{1,0:T(8,128)} %get-tuple-element.4) | data formatting | bytes 2359296
  80.7 0.0 copy-done
  80.8 1.0 %copy.14 = f32[64,4608]{1,0:T(8,128)} copy(f32[64,4608]{1,0:T(8,128)S(1)} %copy-done) | data formatting | bytes 2359296
Async XLA Ops:
  78.3 2.5 %copy-start = (f32[64,4608]{1,0:T(8,128)S(1)}, f32[64,4608]{1,0:T(8,128)}, u32[]{:S(2)}) copy-start(f32[64,4608]{1,0:T(8,128)} %get-tuple-element.5) | copy-start | bytes 3538948
